TPU v7x, 32 devices: a whole 2x2x4 slice. The times are simulated.
32 devices in a mesh: gx: 4 (over z), gy: 4 (over y, x), layer: 2 (over core).
Axes of the slice: x: 2, y: 2, z: 4, core: 2. Of those that a mesh axis runs over, the one named last changes fastest.
Arguments:
- load_current: float32 [8, 64, 2048], P('layer', 'gx', 'gy'), may hold values from -12 to 12
- pad_cond: float32 [8, 64, 2048], P('layer', 'gx', 'gy'), may hold values from 0.01 to 0.1
- cond_x: float32 [8, 64, 2048], P('layer', 'gx', 'gy'), may hold values from 0.5 to 4
- cond_y: float32 [8, 64, 2048], P('layer', 'gx', 'gy'), may hold values from 0.5 to 4
- via_map: int32 [8, 64, 2048], P('layer', 'gx', 'gy'), may hold values from 0 to 3
- branch_index: int32 [4096, 256], P(('gx', 'gy', 'layer')), may hold values from 0 to 7679
- tree_owner: int32 [4096, 1], P(('gx', 'gy', 'layer')), may hold values from 0 to 15; in each aligned block of 128 rows (0 to 127, 128 to 255, ...) at most 16 rows name the same one
- initial_stress: float32 [4096, 256], P(('gx', 'gy', 'layer')), may hold values from -6 to 6
- block_inverse: float32 [16, 256, 256], P(('gx', 'gy')), may hold values from -1.5 to 1.5
Outputs:
- drop: float32 [8, 64, 2048], P('layer', 'gx', 'gy')
- final_stress: float32 [4096, 256], P(('gx', 'gy', 'layer'))
Inputs may be any that keep to these rules, and one draw needn't show every extreme that they name: `tree_owner`: among the 128 trees of one device at most 16 have one owner, and some owner has exactly 16. Owners count in gx+gy order within the tree's own layer group. `branch_index`: A branch joins a node to its next node along x inside the home tile.
All inputs are finite; a program needn't handle non-finite values.
Results may differ from a plain program's by a relative error of at most 0.0003.
Values sent between devices are 32-bit elements; how exact they have to be, the bound alone decides.
A program may use at most 64 MiB of HBM per device.

v0:
```python
import jax
import jax.numpy as jnp
from jax import lax
from jax.sharding import PartitionSpec as P

KX = 2
KY = 4
ITERS = 2
SWEEPS = 4
STEPS = 8
OMEGA = 0.7
TAU = 0.6
VIA_G = 1.5
COARSE_G = 64.0
KAPPA = 2.0


def padded_2(block, sides, width):
    for axis, dim in sides:
        count = lax.axis_size(axis)
        forward = [(i, i + 1) for i in range(count - 1)]
        backward = [(target, source) for source, target in forward]
        low = lax.ppermute(
            lax.slice_in_dim(block, block.shape[dim] - width, None, axis=dim), axis, forward
        )
        high = lax.ppermute(lax.slice_in_dim(block, 0, width, axis=dim), axis, backward)
        block = jnp.concatenate([low, block, high], axis=dim)
    return block


def grid_rims(stacked):
    return padded_2(stacked, (("gx", 2), ("gy", 3), ("layer", 1)), 1)


def total(values):
    return lax.psum(values, ("gx", "gy", "layer"))


def per_device(
    load_current,
    pad_cond,
    cond_x,
    cond_y,
    via_map,
    branch_index,
    tree_owner,
    initial_stress,
    block_inverse,
):
    layers, rows, cols = load_current.shape
    size_x = lax.axis_size("gx")
    size_y = lax.axis_size("gy")
    size_l = lax.axis_size("layer")
    glob_i = lax.axis_index("gx") * rows + jnp.arange(rows, dtype=jnp.int32)
    glob_j = lax.axis_index("gy") * cols + jnp.arange(cols, dtype=jnp.int32)
    glob_l = lax.axis_index("layer") * layers + jnp.arange(layers, dtype=jnp.int32)
    mask_x = (glob_i < rows * size_x - 1).astype(jnp.float32)
    mask_y = (glob_j < cols * size_y - 1).astype(jnp.float32)
    mask_z = (glob_l < layers * size_l - 1).astype(jnp.float32)
    link_x = cond_x * mask_x[None, :, None]
    link_y = cond_y * mask_y[None, None, :]
    link_z = via_map.astype(jnp.float32) * VIA_G * mask_z[:, None, None]
    links = grid_rims(jnp.stack([link_x, link_y, link_z]))
    down_x = links[0, 1:-1, :-2, 1:-1]
    down_y = links[1, 1:-1, 1:-1, :-2]
    down_z = links[2, :-2, 1:-1, 1:-1]
    diag = pad_cond + link_x + down_x + link_y + down_y + link_z + down_z

    def restrict(field):
        return jnp.sum(field.reshape(layers, KX, rows // KX, KY, cols // KY), axis=(0, 2, 4))

    def prolong(coarse):
        spread = jnp.broadcast_to(
            coarse[None, :, None, :, None], (layers, KX, rows // KX, KY, cols // KY)
        )
        return spread.reshape(layers, rows, cols)

    cdiag_own = restrict(pad_cond)

    def collect(small):
        every = lax.all_gather(small.reshape(1, KX * KY), ("gx", "gy", "layer"), axis=0, tiled=True)
        shaped = every.reshape(size_x, size_y, size_l, KX, KY).transpose(2, 0, 3, 1, 4)
        return shaped.reshape(size_l, size_x * KX, size_y * KY)

    cdiag_all = collect(cdiag_own)
    cdiag_full = cdiag_all + 6.0 * COARSE_G

    def coarse_solve(coarse_rhs):
        rhs_all = collect(coarse_rhs)
        value = jnp.zeros_like(rhs_all)
        for sweep in range(SWEEPS):
            padded = jnp.pad(value, 1)
            beside_all = padded[:-2, 1:-1, 1:-1] + padded[2:, 1:-1, 1:-1]
            beside_all = beside_all + padded[1:-1, 2:, 1:-1] + padded[1:-1, :-2, 1:-1]
            beside_all = beside_all + padded[1:-1, 1:-1, 2:] + padded[1:-1, 1:-1, :-2]
            value = (
                value + TAU * (rhs_all - (cdiag_full * value - COARSE_G * beside_all)) / cdiag_full
            )
        start = (lax.axis_index("layer"), lax.axis_index("gx") * KX, lax.axis_index("gy") * KY)
        return lax.dynamic_slice(value, start, (1, KX, KY))[0]

    def precondition(resid):
        return OMEGA * resid / diag + prolong(coarse_solve(restrict(resid)))

    drop = jnp.zeros_like(load_current)
    resid = load_current
    zvec = precondition(resid)
    direction = zvec
    rz_now = total(jnp.sum(resid * zvec))
    for step in range(ITERS):
        operate_padded = grid_rims(direction[None])[0]
        out = pad_cond * direction
        out = (
            out
            + link_x * (direction - operate_padded[1:-1, 2:, 1:-1])
            + down_x * (direction - operate_padded[1:-1, :-2, 1:-1])
        )
        out = (
            out
            + link_y * (direction - operate_padded[1:-1, 1:-1, 2:])
            + down_y * (direction - operate_padded[1:-1, 1:-1, :-2])
        )
        out = (
            out
            + link_z * (direction - operate_padded[2:, 1:-1, 1:-1])
            + down_z * (direction - operate_padded[:-2, 1:-1, 1:-1])
        )
        alpha = rz_now / total(jnp.sum(direction * out))
        drop = drop + alpha * direction
        resid = resid - alpha * out
        if step + 1 < ITERS:
            zvec = precondition(resid)
            rz_next = total(jnp.sum(resid * zvec))
            direction = zvec + rz_next / rz_now * direction
            rz_now = rz_next
    trees_dev, segs = initial_stress.shape
    owners_count = size_x * size_y
    capacity = 2 * trees_dev // owners_count
    seg_layer = (jnp.arange(segs, dtype=jnp.int32) % layers)[None, :]
    cell = seg_layer * (rows * cols) + branch_index
    flat_drop = drop.reshape(-1)
    flat_link = link_x.reshape(-1)
    current = flat_link[cell] * (flat_drop[cell] - flat_drop[cell + cols])
    owners = tree_owner[:, 0]
    hits = (owners[:, None] == jnp.arange(owners_count, dtype=jnp.int32)[None, :]).astype(jnp.int32)
    slot_rank = jnp.sum((jnp.cumsum(hits, axis=0) - hits) * hits, axis=1)
    payload = jnp.stack([current, initial_stress])
    outgoing = (
        jnp.zeros((2, owners_count, capacity, segs), jnp.float32)
        .at[:, owners, slot_rank]
        .set(payload)
    )
    inverse = block_inverse[0]
    piece = lax.all_to_all(outgoing, ("gx", "gy"), split_axis=1, concat_axis=1, tiled=True)
    count = piece.shape[2]
    flow = piece[0].reshape(-1, segs)
    stress = piece[1].reshape(-1, segs)
    for step in range(STEPS):
        stress = jnp.einsum(
            "ts,us->tu", stress + KAPPA * flow, inverse, precision=lax.Precision.HIGHEST
        )
    returning = stress.reshape(owners_count, count, segs)
    solved = lax.all_to_all(returning, ("gx", "gy"), split_axis=0, concat_axis=0, tiled=True)
    final_stress = solved[owners, slot_rank]
    return (drop, final_stress)


def solution(mesh):
    return jax.shard_map(
        per_device,
        mesh=mesh,
        in_specs=(
            P("layer", "gx", "gy"),
            P("layer", "gx", "gy"),
            P("layer", "gx", "gy"),
            P("layer", "gx", "gy"),
            P("layer", "gx", "gy"),
            P(("gx", "gy", "layer"), None),
            P(("gx", "gy", "layer"), None),
            P(("gx", "gy", "layer"), None),
            P(("gx", "gy"), None, None),
        ),
        out_specs=(P("layer", "gx", "gy"), P(("gx", "gy", "layer"), None)),
        check_vma=False,
    )
```

profile of v0, /device:TPU:0, one launch (start us, length us, event | category | flops | bytes accessed | tf_op | source)
XLA Modules:
  0.0 902.8 jit_solution(7220110713637692259)
XLA Ops:
  0.7 1.1 fusion.137
  1.9 4.9 collective-permute-start
  6.9 1.3 collective-permute-start.1
  8.4 42.6 %all-gather.1 = f32[32,1,8]{2,1,0:T(1,128)S(1)} all-gather(f32[1,1,8]{2,1,0:T(1,128)S(1)} %reshape.172), channel_id=1, replica_groups=mesh['gx'=4,'gy'=4,'layer'=2] {'gx','gy','layer'}, dimensions={0}, use_global_device_ids=true | all-gather | bytes 1056 | tf_op jit(solution)/shard_map/all_gather | solution.py:81
  51.5 36.4 %all-gather = f32[32,1,8]{2,1,0:T(1,128)S(1)} all-gather(f32[1,1,8]{2,1,0:T(1,128)S(1)} %reshape.170), channel_id=1, replica_groups=mesh['gx'=4,'gy'=4,'layer'=2] {'gx','gy','layer'}, dimensions={0}, use_global_device_ids=true | all-gather | bytes 1056 | tf_op jit(solution)/shard_map/all_gather | solution.py:81
  87.9 0.5 broadcast.260
  88.4 0.7 reduce.16
  89.6 0.4 copy-done.7
  90.3 3.6 collective-permute-start.2
  93.9 1.3 collective-permute-start.3
  95.3 2.2 collective-permute-done.2
  97.5 4.1 collective-permute-done.3
  101.8 1.3 collective-permute-start.4
  103.2 0.9 collective-permute-done.4
  104.3 1.3 collective-permute-start.5
  105.6 1.3 collective-permute-start.6
  107.0 4.1 collective-permute-done.6
  111.2 3.2 collective-permute-start.7
  114.5 1.3 collective-permute-start.8
  115.8 0.4 collective-permute-done.7
  116.2 4.3 collective-permute-done.8
  120.6 1.3 collective-permute-start.10
  121.9 3.0 collective-permute-start.9
  125.0 0.8 collective-permute-done.9
  125.8 0.2 maximum_bitcast_fusion
  126.0 0.9 multiply_reduce_fusion.1
  126.9 39.2 %all-reduce.7 = (f32[]{:T(128)}, f32[]{:T(128)}) all-reduce(f32[]{:T(128)} %get-tuple-element.3, f32[]{:T(128)} %get-tuple-element.2), channel_id=1, replica_groups=mesh['gx'=4,'gy'=4,'layer'=2] {'gx','gy','layer'}, use_global_device_ids=true, to_apply=%region_5.6 | all-reduce | flops 2 | bytes 16 | tf_op jit(solution)/shard_map/psum | solution.py:36
  167.6 41.0 %all-gather.2 = f32[32,1,8]{2,1,0:T(1,128)S(1)} all-gather(f32[1,1,8]{2,1,0:T(1,128)S(1)} %reshape.174), channel_id=1, replica_groups=mesh['gx'=4,'gy'=4,'layer'=2] {'gx','gy','layer'}, dimensions={0}, use_global_device_ids=true | all-gather | bytes 1056 | tf_op jit(solution)/shard_map/all_gather | solution.py:81
  208.6 0.7 reduce.17
  210.0 0.6 multiply_reduce_fusion
  210.7 37.1 %psum.30 = f32[]{:T(128)} all-reduce(f32[]{:T(128)} %get-tuple-element.8), channel_id=1, replica_groups=mesh['gx'=4,'gy'=4,'layer'=2] {'gx','gy','layer'}, use_global_device_ids=true, to_apply=%region_11.12 | all-reduce | flops 1 | bytes 8 | tf_op jit(solution)/shard_map/psum | solution.py:36
  249.0 4.8 collective-permute-start.11
  253.8 1.3 collective-permute-start.12
  255.4 4.0 collective-permute-done.12
  259.4 4.2 collective-permute-start.13
  263.6 1.3 collective-permute-start.14
  265.1 0.3 collective-permute-done.13
  265.4 4.3 collective-permute-done.14
  269.7 1.3 collective-permute-start.15
  271.0 1.3 collective-permute-start.16
  272.4 1.8 collective-permute-done.16
  274.2 0.2 maximum_bitcast_fusion.1
  274.4 0.9 fusion.22
  275.2 180.5 %gather_fusion = f32[32768]{0:T(1024)S(1)} fusion(f32[32768]{0:T(1024)S(1)} %bitcast.94, s32[32768]{0:T(1024)S(1)} %broadcast_clamp_fusion.1), kind=kCustom, calls=%fused_computation | custom fusion | bytes 393216 | tf_op jit(solution)/shard_map/gather | solution.py:143
  455.8 39.4 %psum.31 = f32[]{:T(128)} all-reduce(f32[]{:T(128)} %fusion.22), channel_id=1, replica_groups=mesh['gx'=4,'gy'=4,'layer'=2] {'gx','gy','layer'}, use_global_device_ids=true, to_apply=%region_13.14 | all-reduce | flops 1 | bytes 8 | tf_op jit(solution)/shard_map/psum | solution.py:36
  496.6 0.6 copy-done.6
  497.2 180.5 %gather_fusion.1 = f32[32768]{0:T(1024)S(1)} fusion(f32[32768]{0:T(1024)S(1)} %bitcast.92, s32[32768]{0:T(1024)S(1)} %broadcast_clamp_fusion.1), kind=kCustom, calls=%fused_computation.1 | custom fusion | bytes 393216 | tf_op jit(solution)/shard_map/gather | solution.py:143
  677.7 180.5 %gather_fusion.2 = f32[32768]{0:T(1024)S(1)} fusion(f32[32768]{0:T(1024)S(1)} %bitcast.93, s32[32768]{0:T(1024)S(1)} %broadcast_clamp_fusion), kind=kCustom, calls=%fused_computation.2 | custom fusion | bytes 393216 | tf_op jit(solution)/shard_map/gather | solution.py:143
  858.4 0.8 copy-done.8
  859.2 0.2 copy.27
  859.4 0.2 broadcast_in_dim.57
  859.6 5.7 scatter_fusion
  865.4 19.4 %all_to_all.10 = f32[2,16,16,256]{3,0,2,1:T(2,128)S(1)} all-to-all(f32[2,16,16,256]{3,0,2,1:T(2,128)S(1)} %scatter_fusion), channel_id=1, replica_groups=mesh['gx'=4,'gy'=4,'layer'=2] {'gx','gy'}, dimensions={1} | all-to-all | bytes 1048576 | tf_op jit(solution)/shard_map/all_to_all | solution.py:154
  884.7 0.6 slice_add_fusion
  885.4 0.4 convolution_add_fusion.6
  885.8 0.4 convolution_add_fusion.5
  886.2 0.4 convolution_add_fusion.4
  886.6 0.4 convolution_add_fusion.3
  887.1 0.4 convolution_add_fusion.2
  887.5 0.4 convolution_add_fusion.1
  887.9 0.4 convolution_add_fusion
  888.3 0.4 fusion
  888.7 12.1 %all_to_all.11 = f32[16,16,256]{2,1,0:T(8,128)S(1)} all-to-all(f32[16,16,256]{2,1,0:T(8,128)S(1)} %fusion), channel_id=1, replica_groups=mesh['gx'=4,'gy'=4,'layer'=2] {'gx','gy'}, dimensions={0} | all-to-all | bytes 524288 | tf_op jit(solution)/shard_map/all_to_all | solution.py:163
  900.9 1.9 gather_fusion.3
  (89 shorter events, 4.3 us)
Async XLA Ops:
  0.6 884.7 %copy-start = (f32[1,256,256]{2,1,0:T(8,128)S(1)}, f32[1,256,256]{2,1,0:T(8,128)}, u32[]{:S(2)}) copy-start(f32[1,256,256]{2,1,0:T(8,128)} %param.17) | copy-start | bytes 786436
  0.7 1.1 copy-start.4
  0.7 1.1 copy-start.5
  1.9 6.3 copy-start.3
  1.9 88.2 %collective-permute-start = (f32[3,4,1,512]{3,2,1,0:T(1,128)S(1)}, f32[3,4,1,512]{3,2,1,0:T(1,128)S(1)}, u32[]{:S(2)}, u32[]{:S(2)}) collective-permute-start(f32[3,4,1,512]{3,2,1,0:T(1,128)S(1)} %get-tuple-element.23), channel_id=1, source_target_pairs={{0,8},{8,16},{16,24},{1,9},{9,17},{17,25},{2,10},{10,18},{18,26},{... | collective-permute-start | bytes 73736 | tf_op jit(solution)/shard_map/ppermute | solution.py:23
  6.9 83.3 %collective-permute-start.1 = (f32[3,4,1,512]{3,2,1,0:T(1,128)S(1)}, f32[3,4,1,512]{3,2,1,0:T(1,128)S(1)}, u32[]{:S(2)}, u32[]{:S(2)}) collective-permute-start(f32[3,4,1,512]{3,2,1,0:T(1,128)S(1)} %get-tuple-element.22), channel_id=1, source_target_pairs={{8,0},{16,8},{24,16},{9,1},{17,9},{25,17},{10,2},{18,10},{26,18},{... | collective-permute-start | bytes 73736 | tf_op jit(solution)/shard_map/ppermute | solution.py:26
  8.2 43.1 %copy-start.2 = (f32[4,16,512]{2,1,0:T(8,128)S(1)}, f32[4,16,512]{2,1,0:T(8,128)}, u32[]{:S(2)}) copy-start(f32[4,16,512]{2,1,0:T(8,128)} %param.9) | copy-start | bytes 393220
  89.1 0.9 copy-start.7
  90.3 7.2 collective-permute-start.2
  93.9 7.7 collective-permute-start.3
  101.8 2.3 collective-permute-start.4
  103.1 1.0 copy-start.1
  104.3 2.7 collective-permute-start.5
  105.6 5.6 collective-permute-start.6
  111.2 4.9 collective-permute-start.7
  114.5 6.0 collective-permute-start.8
  120.6 4.4 collective-permute-start.10
  121.9 3.9 collective-permute-start.9
  249.0 6.4 collective-permute-start.11
  253.8 1.3 copy-start.9
  253.8 5.5 collective-permute-start.12
  259.4 5.9 collective-permute-start.13
  263.6 6.0 collective-permute-start.14
  269.7 2.7 collective-permute-start.15
  271.0 3.1 collective-permute-start.16
  496.5 0.7 copy-start.6
  858.3 0.9 copy-start.8
where the time goes:
time: 904 us; the launch traced here: 903 us
  local copies, waits for them, and re-layouts  553 us (61%)
  blocking collectives  267 us (30%)
  starting transfers between devices  38 us (4%)
  waiting for transfers between devices  27 us (3%)
    gather x3, local copies, waits for them, and re-layouts, per_device(): current = flat_link[cell] * (flat_drop[cell] - flat_drop[cell + cols])  542 us
    all_gather x3, blocking collectives, collect(): lax.all_gather(small.reshape(1, KX * KY), ('gx', 'gy', 'layer'), axis=0,...  120 us
    psum x3, blocking collectives, total(): return lax.psum(values, ('gx', 'gy', 'layer'))  116 us
    ppermute x9, starting transfers between devices, padded_2(): lax.ppermute(lax.slice_in_dim(block, block.shape[dim] - width, None, axis...  27.6 us
    ppermute x8, waiting for transfers between devices, padded_2(): lax.ppermute(lax.slice_in_dim(block, 0, width, axis=dim), axis, backward)  22.5 us
    all_to_all x1, blocking collectives, per_device(): lax.all_to_all(outgoing, ('gx', 'gy'), split_axis=1, concat_axis=1, tiled...  19.4 us
  transfers between devices with their start and end apart: 17, of which 11 were waited for; matrix products, arithmetic and copies ran while one was open for 0% of the time, Pallas kernels for 0%

commit v1 on v0

--- a/solution.py
+++ b/solution.py
@@ -33,7 +33,7 @@
 
 
 def total(values):
-    return lax.psum(values, ("gx", "gy", "layer"))
+    return lax.psum(lax.psum(values, ("gy", "layer")), "gx")
 
 
 def per_device(

time: 904 us -> 847 us (0.937)
  blocking collectives: 267 us -> 214 us
    psum x3 -> x6, blocking collectives: 116 us -> 68 us  [total(): return lax.psum(lax.psum(values, ('gy', 'layer')), 'gx')]
where the time goes in v1:
time: 847 us
  local copies, waits for them, and re-layouts  553 us (65%)
  blocking collectives  214 us (25%)
  starting transfers between devices  33.3 us (4%)
  waiting for transfers between devices  29 us (3%)
  other arithmetic  8.71 us (1%)
    gather x3, local copies, waits for them, and re-layouts, per_device(): current = flat_link[cell] * (flat_drop[cell] - flat_drop[cell + cols])  542 us
    all_gather x3, blocking collectives, collect(): lax.all_gather(small.reshape(1, KX * KY), ('gx', 'gy', 'layer'), axis=0,...  116 us
    psum x6, blocking collectives, total(): return lax.psum(lax.psum(values, ('gy', 'layer')), 'gx')  68 us
    ppermute x8, waiting for transfers between devices, padded_2(): lax.ppermute(lax.slice_in_dim(block, 0, width, axis=dim), axis, backward)  24.4 us
    ppermute x9, starting transfers between devices, padded_2(): lax.ppermute(lax.slice_in_dim(block, block.shape[dim] - width, None, axis...  23 us
    all_to_all x1, blocking collectives, per_device(): lax.all_to_all(outgoing, ('gx', 'gy'), split_axis=1, concat_axis=1, tiled...  18.3 us
  transfers between devices with their start and end apart: 17, of which 11 were waited for; matrix products, arithmetic and copies ran while one was open for 0% of the time, Pallas kernels for 0%

profile of v1, /device:TPU:0, one launch (start us, length us, event | category | flops | bytes accessed | tf_op | source)
XLA Modules:
  0.0 846.6 jit_solution(3146672086973170022)
XLA Ops:
  0.7 1.1 fusion.137
  1.9 4.9 collective-permute-start
  6.9 1.3 collective-permute-start.1
  8.4 42.6 %all-gather.1 = f32[32,1,8]{2,1,0:T(1,128)S(1)} all-gather(f32[1,1,8]{2,1,0:T(1,128)S(1)} %reshape.172), channel_id=1, replica_groups=mesh['gx'=4,'gy'=4,'layer'=2] {'gx','gy','layer'}, dimensions={0}, use_global_device_ids=true | all-gather | bytes 1056 | tf_op jit(solution)/shard_map/all_gather | solution.py:81
  51.5 36.4 %all-gather = f32[32,1,8]{2,1,0:T(1,128)S(1)} all-gather(f32[1,1,8]{2,1,0:T(1,128)S(1)} %reshape.170), channel_id=1, replica_groups=mesh['gx'=4,'gy'=4,'layer'=2] {'gx','gy','layer'}, dimensions={0}, use_global_device_ids=true | all-gather | bytes 1056 | tf_op jit(solution)/shard_map/all_gather | solution.py:81
  87.9 0.5 broadcast.260
  88.4 0.7 reduce.16
  89.9 3.6 collective-permute-start.2
  93.5 1.3 collective-permute-start.3
  94.9 2.2 collective-permute-done.2
  97.1 4.1 collective-permute-done.3
  101.3 1.3 collective-permute-start.4
  102.7 1.0 collective-permute-done.4
  103.9 1.3 collective-permute-start.5
  105.2 1.3 collective-permute-start.6
  106.6 4.1 collective-permute-done.6
  110.8 3.2 collective-permute-start.7
  114.0 1.3 collective-permute-start.8
  115.4 0.3 collective-permute-done.7
  115.8 4.3 collective-permute-done.8
  120.2 1.3 collective-permute-start.10
  121.5 3.0 collective-permute-start.9
  124.5 0.8 collective-permute-done.9
  125.6 0.9 multiply_reduce_fusion.1
  126.4 12.9 %all-reduce.7 = (f32[]{:T(128)}, f32[]{:T(128)}) all-reduce(f32[]{:T(128)} %get-tuple-element.3, f32[]{:T(128)} %get-tuple-element.2), channel_id=1, replica_groups=mesh['gx'=4,'gy'=4,'layer'=2] {'gy','layer'}, use_global_device_ids=true, to_apply=%region_5.6 | all-reduce | flops 2 | bytes 16 | tf_op jit(solution)/shard_map/psum | solution.py:36
  139.3 10.2 %all-reduce.8 = (f32[]{:T(128)}, f32[]{:T(128)}) all-reduce(f32[]{:T(128)} %get-tuple-element.4, f32[]{:T(128)} %get-tuple-element.5), channel_id=1, replica_groups=mesh['gx'=4,'gy'=4,'layer'=2] {'gx'}, use_global_device_ids=true, to_apply=%region_6.7 | all-reduce | flops 2 | bytes 16 | tf_op jit(solution)/shard_map/psum | solution.py:36
  151.0 36.7 %all-gather.2 = f32[32,1,8]{2,1,0:T(1,128)S(1)} all-gather(f32[1,1,8]{2,1,0:T(1,128)S(1)} %reshape.174), channel_id=1, replica_groups=mesh['gx'=4,'gy'=4,'layer'=2] {'gx','gy','layer'}, dimensions={0}, use_global_device_ids=true | all-gather | bytes 1056 | tf_op jit(solution)/shard_map/all_gather | solution.py:81
  187.6 0.7 reduce.17
  189.0 0.7 multiply_reduce_fusion
  189.7 12.7 %psum.60 = f32[]{:T(128)} all-reduce(f32[]{:T(128)} %get-tuple-element.10), channel_id=1, replica_groups=mesh['gx'=4,'gy'=4,'layer'=2] {'gy','layer'}, use_global_device_ids=true, to_apply=%region_13.14 | all-reduce | flops 1 | bytes 8 | tf_op jit(solution)/shard_map/psum | solution.py:36
  202.4 10.6 %psum.61 = f32[]{:T(128)} all-reduce(f32[]{:T(128)} %psum.60), channel_id=1, replica_groups=mesh['gx'=4,'gy'=4,'layer'=2] {'gx'}, use_global_device_ids=true, to_apply=%region_14.15 | all-reduce | flops 1 | bytes 8 | tf_op jit(solution)/shard_map/psum | solution.py:36
  214.4 2.3 collective-permute-start.11
  216.7 1.3 collective-permute-start.12
  218.2 4.0 collective-permute-done.12
  222.3 2.0 collective-permute-start.13
  224.3 1.3 collective-permute-start.14
  225.8 0.3 collective-permute-done.13
  226.1 6.1 collective-permute-done.14
  232.3 1.3 collective-permute-start.15
  233.6 1.3 collective-permute-start.16
  234.9 1.8 collective-permute-done.16
  236.9 0.9 fusion.22
  237.8 12.6 %psum.62 = f32[]{:T(128)} all-reduce(f32[]{:T(128)} %fusion.22), channel_id=1, replica_groups=mesh['gx'=4,'gy'=4,'layer'=2] {'gy','layer'}, use_global_device_ids=true, to_apply=%region_16.17 | all-reduce | flops 1 | bytes 8 | tf_op jit(solution)/shard_map/psum | solution.py:36
  250.4 180.5 %gather_fusion = f32[32768]{0:T(1024)S(1)} fusion(f32[32768]{0:T(1024)S(1)} %bitcast.94, s32[32768]{0:T(1024)S(1)} %broadcast_clamp_fusion.1), kind=kCustom, calls=%fused_computation | custom fusion | bytes 393216 | tf_op jit(solution)/shard_map/gather | solution.py:143
  430.9 9.0 %psum.63 = f32[]{:T(128)} all-reduce(f32[]{:T(128)} %psum.62), channel_id=1, replica_groups=mesh['gx'=4,'gy'=4,'layer'=2] {'gx'}, use_global_device_ids=true, to_apply=%region_17.18 | all-reduce | flops 1 | bytes 8 | tf_op jit(solution)/shard_map/psum | solution.py:36
  441.4 0.6 copy-done.6
  442.0 180.5 %gather_fusion.1 = f32[32768]{0:T(1024)S(1)} fusion(f32[32768]{0:T(1024)S(1)} %bitcast.92, s32[32768]{0:T(1024)S(1)} %broadcast_clamp_fusion.1), kind=kCustom, calls=%fused_computation.1 | custom fusion | bytes 393216 | tf_op jit(solution)/shard_map/gather | solution.py:143
  622.5 180.5 %gather_fusion.2 = f32[32768]{0:T(1024)S(1)} fusion(f32[32768]{0:T(1024)S(1)} %bitcast.93, s32[32768]{0:T(1024)S(1)} %broadcast_clamp_fusion), kind=kCustom, calls=%fused_computation.2 | custom fusion | bytes 393216 | tf_op jit(solution)/shard_map/gather | solution.py:143
  803.2 0.8 copy-done.8
  804.1 0.2 copy.27
  804.3 0.2 broadcast_in_dim.57
  804.5 5.7 scatter_fusion
  810.2 18.3 %all_to_all.10 = f32[2,16,16,256]{3,0,2,1:T(2,128)S(1)} all-to-all(f32[2,16,16,256]{3,0,2,1:T(2,128)S(1)} %scatter_fusion), channel_id=1, replica_groups=mesh['gx'=4,'gy'=4,'layer'=2] {'gx','gy'}, dimensions={1} | all-to-all | bytes 1048576 | tf_op jit(solution)/shard_map/all_to_all | solution.py:154
  828.5 0.6 slice_add_fusion
  829.1 0.4 convolution_add_fusion.6
  829.5 0.4 convolution_add_fusion.5
  829.9 0.4 convolution_add_fusion.4
  830.4 0.4 convolution_add_fusion.3
  830.8 0.4 convolution_add_fusion.2
  831.2 0.4 convolution_add_fusion.1
  831.6 0.4 convolution_add_fusion
  832.0 0.4 fusion
  832.5 12.2 %all_to_all.11 = f32[16,16,256]{2,1,0:T(8,128)S(1)} all-to-all(f32[16,16,256]{2,1,0:T(8,128)S(1)} %fusion), channel_id=1, replica_groups=mesh['gx'=4,'gy'=4,'layer'=2] {'gx','gy'}, dimensions={0} | all-to-all | bytes 524288 | tf_op jit(solution)/shard_map/all_to_all | solution.py:163
  844.7 1.9 gather_fusion.3
  (92 shorter events, 4.7 us)
Async XLA Ops:
  0.6 828.5 %copy-start = (f32[1,256,256]{2,1,0:T(8,128)S(1)}, f32[1,256,256]{2,1,0:T(8,128)}, u32[]{:S(2)}) copy-start(f32[1,256,256]{2,1,0:T(8,128)} %param.17) | copy-start | bytes 786436
  0.7 1.1 copy-start.4
  0.7 1.1 copy-start.5
  1.9 6.3 copy-start.3
  1.9 87.8 %collective-permute-start = (f32[3,4,1,512]{3,2,1,0:T(1,128)S(1)}, f32[3,4,1,512]{3,2,1,0:T(1,128)S(1)}, u32[]{:S(2)}, u32[]{:S(2)}) collective-permute-start(f32[3,4,1,512]{3,2,1,0:T(1,128)S(1)} %get-tuple-element.25), channel_id=1, source_target_pairs={{0,8},{8,16},{16,24},{1,9},{9,17},{17,25},{2,10},{10,18},{18,26},{... | collective-permute-start | bytes 73736 | tf_op jit(solution)/shard_map/ppermute | solution.py:23
  6.9 82.9 %collective-permute-start.1 = (f32[3,4,1,512]{3,2,1,0:T(1,128)S(1)}, f32[3,4,1,512]{3,2,1,0:T(1,128)S(1)}, u32[]{:S(2)}, u32[]{:S(2)}) collective-permute-start(f32[3,4,1,512]{3,2,1,0:T(1,128)S(1)} %get-tuple-element.24), channel_id=1, source_target_pairs={{8,0},{16,8},{24,16},{9,1},{17,9},{25,17},{10,2},{18,10},{26,18},{... | collective-permute-start | bytes 73736 | tf_op jit(solution)/shard_map/ppermute | solution.py:26
  8.2 43.1 %copy-start.2 = (f32[4,16,512]{2,1,0:T(8,128)S(1)}, f32[4,16,512]{2,1,0:T(8,128)}, u32[]{:S(2)}) copy-start(f32[4,16,512]{2,1,0:T(8,128)} %param.9) | copy-start | bytes 393220
  89.9 7.2 collective-permute-start.2
  93.5 7.7 collective-permute-start.3
  94.9 8.8 %copy-start.1 = (f32[4,16,512]{2,1,0:T(8,128)S(1)}, f32[4,16,512]{2,1,0:T(8,128)}, u32[]{:S(2)}) copy-start(f32[4,16,512]{2,1,0:T(8,128)} %param.11) | copy-start | bytes 393220
  101.3 2.3 collective-permute-start.4
  102.7 3.8 copy-start.7
  103.9 2.7 collective-permute-start.5
  105.2 5.6 collective-permute-start.6
  110.8 4.9 collective-permute-start.7
  114.0 6.0 collective-permute-start.8
  120.2 4.4 collective-permute-start.10
  121.5 3.9 collective-permute-start.9
  214.4 3.9 collective-permute-start.11
  216.6 1.3 copy-start.9
  216.7 5.5 collective-permute-start.12
  222.3 3.8 collective-permute-start.13
  224.3 7.8 collective-permute-start.14
  232.3 2.6 collective-permute-start.15
  233.6 3.1 collective-permute-start.16
  441.3 0.7 copy-start.6
  803.1 0.9 copy-start.8
